TPU v7x, 256 devices: a whole 4x4x8 slice. The times are simulated.
256 devices in a mesh: dp: 16 (over z, y_hi), mp: 16 (over x, y_lo, core).
Axes of the slice: x: 4, y: 4 (y_hi: 2, y_lo: 2; y = y_hi * 2 + y_lo), z: 8, core: 2. Of those that a mesh axis runs over, the one named last changes fastest.
Arguments:
- grad_parts: bfloat16 [16, 1024, 16384], P('dp', None, 'mp'), may hold values from -24 to 24
- params: bfloat16 [1024, 16384], P('dp', 'mp'), may hold values from -6 to 6
- stale_left: bfloat16 [16, 1024, 1024], P('mp'), may hold values from -1 to 2
- stale_right: bfloat16 [16, 1024, 1024], P('mp'), may hold values from -1 to 2
- step_matrix: int32 [16], replicated, may hold values from 0 to 31, as said below
Outputs:
- new_params: float32 [1024, 16384], P('dp', 'mp')
- left_roots: bfloat16 [16, 1024, 1024], P('mp', 'dp')
- right_roots: bfloat16 [16, 1024, 1024], P('mp', 'dp')
Inputs may be any that keep to these rules, and one draw needn't show every extreme that they name: The 16 entries are distinct. Owner o refreshes statistic step_matrix[o]: that of block step_matrix[o] // 2, the left one if the entry is even, the right one if it is odd. A block may have none, one or both of its statistics refreshed.
All inputs are finite; a program needn't handle non-finite values.
Results may differ from a plain program's by a relative error of at most 0.0045.
Values may be sent and summed in bfloat16 or wider, within the bound.
A program may use at most 128 MiB of HBM per device.

v0:
```python
import jax
import jax.numpy as jnp
from jax import lax
from jax.sharding import PartitionSpec as P

ITERS = 2


EPS = 1e-06
DAMP = 0.05
STEP_SIZE = 0.5
HIGH = lax.Precision.HIGHEST


def batched(left, right):
    return jnp.einsum(
        "sij,sjk->sik", left, right, precision=HIGH, preferred_element_type=jnp.float32
    )


def per_device(grad_parts, params, stale_left, stale_right, step_matrix):
    block = grad_parts[0]
    width = block.shape[0]
    groups = lax.axis_size("dp")
    owners = lax.axis_size("mp")
    rows = width // groups
    row_at = lax.axis_index("dp") * rows
    owner = lax.axis_index("mp")
    chosen = step_matrix[owner]
    ident_rows = (
        lax.broadcasted_iota(jnp.int32, (rows, width), 0) + row_at
        == lax.broadcasted_iota(jnp.int32, (rows, width), 1)
    ).astype(jnp.float32)
    ident_full = jnp.eye(width, dtype=jnp.float32)
    left_part = lax.dot_general(
        block, block, (((1,), (1,)), ((), ())), preferred_element_type=jnp.float32
    )
    right_part = lax.dot_general(
        block, block, (((0,), (0,)), ((), ())), preferred_element_type=jnp.float32
    )
    slab = lax.psum_scatter(
        jnp.concatenate([left_part, right_part], axis=1), "dp", scatter_dimension=0, tiled=True
    )

    def stale_rows(stale):
        return lax.dynamic_slice_in_dim(stale[0], row_at, rows, 0)

    def refreshed(target, stale, shared):
        hit = step_matrix == target
        fresh = jnp.sum(
            jnp.where(hit[:, None, None], shared.astype(jnp.float32), jnp.float32(0.0)), axis=0
        ).astype(jnp.bfloat16)
        return jnp.where(jnp.any(hit), fresh, stale_rows(stale))[None]

    whole = lax.all_gather(slab, "mp", axis=0, tiled=True)
    source = lax.dynamic_slice_in_dim(whole, chosen // 2 * rows, rows, 0)
    picked = lax.dynamic_slice_in_dim(source, chosen % 2 * width, width, 1)
    starts = picked[None]
    diag_part = jnp.sum(starts * ident_rows[None], axis=(1, 2))
    total = lax.psum(diag_part, "dp")
    scale = 2.0 * total / width + EPS
    current = starts / scale[:, None, None] + DAMP * ident_rows[None]
    root_rows = ident_rows[None]
    for step in range(ITERS):
        factor = (5.0 * ident_rows[None] - current) * 0.25
        everyone = lax.all_gather(factor, "dp", axis=1, tiled=True)
        root_rows = batched(root_rows, everyone)
        power = batched(factor, everyone)
        power = batched(power, everyone)
        power = batched(power, everyone)
        current = batched(power, 5.0 * ident_full[None] - 4.0 * everyone)
    packed = root_rows.astype(jnp.bfloat16)[0]
    shared = lax.all_gather(packed, "mp", axis=0, tiled=True).reshape(owners, rows, width)
    left_out = refreshed(2 * owner, stale_left, shared)
    right_out = refreshed(2 * owner + 1, stale_right, shared)
    projected = jnp.dot(block, stale_right[0], preferred_element_type=jnp.float32).astype(
        jnp.bfloat16
    )
    left_matrix = stale_left[0]
    update = lax.psum_scatter(
        jnp.dot(left_matrix, projected, preferred_element_type=jnp.float32) / groups,
        "dp",
        scatter_dimension=0,
        tiled=True,
    )
    new_params = params.astype(jnp.float32) - STEP_SIZE * update
    return (new_params, left_out, right_out)


def solution(mesh):
    return jax.shard_map(
        per_device,
        mesh=mesh,
        in_specs=(
            P("dp", None, "mp"),
            P("dp", "mp"),
            P("mp", None, None),
            P("mp", None, None),
            P(),
        ),
        out_specs=(P("dp", "mp"), P("mp", "dp", None), P("mp", "dp", None)),
        check_vma=False,
    )
```

profile of v0, /device:TPU:6, one launch (start us, length us, event | category | flops | bytes accessed | tf_op | source)
XLA Modules:
  0.0 822.9 jit_solution(1090935723276704376)
XLA Ops:
  7.2 1.5 copy-done
  8.8 2.4 fusion.11
  11.1 2.4 fusion.9
  13.5 4.1 pad_maximum_fusion
  17.6 9.2 %copy.17 = f32[1024,2048]{1,0:T(8,128)} copy(f32[1024,2048]{0,1:T(8,128)} %pad_maximum_fusion) | data formatting | bytes 16777216
  26.8 226.0 %reduce-scatter.9.cloned.1.call-done = f32[64,2048]{1,0:T(8,128)} async-done(((f32[1024,2048]{1,0:T(8,128)}), f32[64,2048]{1,0:T(8,128)}) %reduce-scatter.9.cloned.1.call-update) | async-done | bytes 524304 | tf_op jit(solution)/shard_map/reduce_scatter | solution.py:41
  256.1 51.5 %all-gather.7.cloned.1.call-done = f32[1024,2048]{1,0:T(8,128)} async-done(((f32[64,2048]{1,0:T(8,128)}), f32[1024,2048]{1,0:T(8,128)}) %all-gather.7.cloned.1.call-update) | async-done | bytes 8388624 | tf_op jit(solution)/shard_map/all_gather | solution.py:55
  307.7 1.7 select_reduce_fusion
  309.4 42.7 %psum.7 = f32[1]{0:T(128)} all-reduce(f32[1]{0:T(128)} %bitcast.6), channel_id=1, replica_groups=mesh['dp'=16,'mp'=16] {'dp'}, use_global_device_ids=true, to_apply=%region_4.5 | all-reduce | flops 1 | bytes 8 | tf_op jit(solution)/shard_map/psum | solution.py:60
  352.7 1.8 fusion.32
  354.8 96.6 %all-gather.11.cloned.1.call-done = f32[1024,1024]{1,0:T(8,128)} async-done(((f32[64,1024]{1,0:T(8,128)}), f32[1024,1024]{1,0:T(8,128)}) %all-gather.11.cloned.1.call-update) | async-done | bytes 4194320 | tf_op jit(solution)/shard_map/all_gather | solution.py:66
  451.5 5.1 fusion.42
  456.6 2.6 fusion.43
  459.2 2.6 fusion.44
  461.9 3.6 fusion.21
  465.8 8.7 %multiply_bitcast_fusion = f32[1024,1024]{0,1:T(8,128)} fusion(bf16[1,1024,1024]{2,1,0:T(8,128)(2,1)} %param.7, bf16[1,1024,1024]{2,1,0:T(8,128)(2,1)} %param.8, bf16[1,1024,1024]{2,1,0:T(8,128)(2,1)S(1)} %copy-done), kind=kOutput, calls=%fused_computation.11 | convolution fusion | flops 4297064448 | bytes 10485760 | tf_op jit(solution)/shard_map/dot_general | solution.py:81
  474.4 5.4 copy.15
  479.9 4.0 fusion.34
  483.9 78.3 %all-gather.13.cloned.1.call-done = f32[1024,1024]{1,0:T(8,128)} async-done(((f32[64,1024]{1,0:T(8,128)}), f32[1024,1024]{1,0:T(8,128)}) %all-gather.13.cloned.1.call-update) | async-done | bytes 4194320 | tf_op jit(solution)/shard_map/all_gather | solution.py:66
  562.2 5.5 convolution_convert_fusion
  568.6 206.0 %reduce-scatter.7.cloned.1.call-done = f32[64,1024]{1,0:T(8,128)} async-done(((f32[1024,1024]{1,0:T(8,128)}), f32[64,1024]{1,0:T(8,128)}) %reduce-scatter.7.cloned.1.call-update) | async-done | bytes 262160
  776.7 33.8 %all-gather.9.cloned.1.call-done = bf16[1024,1024]{1,0:T(8,128)(2,1)} async-done(((bf16[64,1024]{1,0:T(8,128)(2,1)}), bf16[1024,1024]{1,0:T(8,128)(2,1)}) %all-gather.9.cloned.1.call-update) | async-done | bytes 2097168 | tf_op jit(solution)/shard_map/all_gather | solution.py:73
  810.5 2.5 fusion.1
  813.0 3.0 bitcast_select_fusion
  (26 shorter events, 4.3 us)
Async XLA Ops:
  7.2 1.6 copy-start
  7.2 245.6 %reduce-scatter.9.cloned.1.call-start = ((), (), s32[]{:S(2)}) async-start(), calls=%async_computation.7 | async-start | bytes 8912896 | tf_op jit(solution)/shard_map/reduce_scatter | solution.py:41
  26.7 226.1 %copy-start.3 = (s32[16]{0:T(128)S(1)}, s32[16]{0:T(128)}, u32[]{:S(2)}) copy-start(s32[16]{0:T(128)} %param.9) | copy-start | bytes 196
  26.8 280.9 %all-gather.7.cloned.1.call-start = ((), (), s32[]{:S(2)}) async-start(), calls=%async_computation.2 | async-start | bytes 8912896 | tf_op jit(solution)/shard_map/all_gather | solution.py:55
  252.8 198.7 %all-gather.11.cloned.1.call-start = ((), (), s32[]{:S(2)}) async-start(), calls=%async_computation.4 | async-start | bytes 4456448 | tf_op jit(solution)/shard_map/all_gather | solution.py:66
  354.6 207.6 %all-gather.13.cloned.1.call-start = ((), (), s32[]{:S(2)}) async-start(), calls=%async_computation.5 | async-start | bytes 4456448 | tf_op jit(solution)/shard_map/all_gather | solution.py:66
  451.5 5.1 copy-start.1
  465.5 309.1 %reduce-scatter.7.cloned.1.call-start = ((), (), s32[]{:S(2)}) async-start(), calls=%async_computation.6 | async-start | bytes 4456448
  479.9 87.8 %copy-start.2 = (bf16[64,1024]{1,0:T(8,128)(2,1)S(1)}, bf16[64,1024]{1,0:T(8,128)(2,1)}, u32[]{:S(2)}) copy-start(bf16[64,1024]{1,0:T(8,128)(2,1)} %param.6) | copy-start | bytes 393220
  479.9 330.6 %all-gather.9.cloned.1.call-start = ((), (), s32[]{:S(2)}) async-start(), calls=%async_computation.3 | async-start | bytes 2228224 | tf_op jit(solution)/shard_map/all_gather | solution.py:73
Sparse Core Ops, SparseCore 0:
  26.9 225.8 reduce-scatter.8
  254.7 52.9 all-gather.6
  354.7 96.7 all-gather.10
  465.6 96.5 all-gather.12
  566.0 208.5 reduce-scatter.6
  777.0 33.4 all-gather.8
where the time goes:
time: 826 us; the launch traced here: 823 us
  waiting for transfers between devices  692 us (84%)
  blocking collectives  42.7 us (5%)
  matrix products  36.8 us (4%)
  local copies, waits for them, and re-layouts  18.9 us (2%)
  between operations  17.5 us (2%)
  other arithmetic  13.9 us (2%)
    reduce_scatter x1, waiting for transfers between devices, per_device(): lax.psum_scatter(jnp.concatenate([left_part, right_part], axis=1), 'dp',...  226 us
    unnamed x7, waiting for transfers between devices  206 us
    all_gather x2, waiting for transfers between devices, per_device(): everyone = lax.all_gather(factor, 'dp', axis=1, tiled=True)  175 us
    all_gather x1, waiting for transfers between devices, per_device(): whole = lax.all_gather(slab, 'mp', axis=0, tiled=True)  51.5 us
    psum x1, blocking collectives, per_device(): total = lax.psum(diag_part, 'dp')  42.7 us
    all_gather x1, waiting for transfers between devices, per_device(): lax.all_gather(packed, 'mp', axis=0, tiled=True)  33.8 us
    dot_general x6, matrix products, batched(): jnp.einsum('sij,sjk->sik', left, right, precision=HIGH, preferred_element...  23.4 us
    unnamed x13, local copies, waits for them, and re-layouts  18.3 us
  transfers between devices with their start and end apart: 6, of which 6 were waited for; matrix products, arithmetic and copies ran while one was open for 3% of the time, Pallas kernels for 0%

commit v1 on v0

v1 whole, which is shorter than its diff:
```python
import functools

import jax
import jax.numpy as jnp
from jax import lax
from jax.experimental import pallas as pl
from jax.experimental.pallas import tpu as pltpu
from jax.sharding import PartitionSpec as P

EPS = 1e-06
DAMP = 0.05
STEP_SIZE = 0.5
RING = 8
PLANES = 2
TILE = 128
PACKED = 5 * TILE
DISTANCES = (4, 3, -3, 2, -2, 1, -1, 0)
SLOT = {distance: slot for slot, distance in enumerate(DISTANCES)}
F32 = jnp.float32
BF16 = jnp.bfloat16
UP, DOWN = 0, 1


def remote(src, dst, sems, at, device):
    return pltpu.make_async_remote_copy(
        src_ref=src,
        dst_ref=dst,
        send_sem=sems[0].at[at],
        recv_sem=sems[1].at[at],
        device_id=device,
        device_id_type=pl.DeviceIdType.MESH,
    )


def tile_at(index):
    return pl.ds(pl.multiple_of(index * TILE, TILE), TILE)


def kernel(
    g_hbm, left_hbm, right_hbm, update_out, roots_out,
    both, left, right, mine, other, lg, lg_tmp,
    mz_send, mz_recv, oz_send, oz_recv, uy_send, uy_recv, uz_send, uz_recv,
    swap_send, swap_recv, packed, full, root_rows, root_recv,
    load_sem, mz_ss, mz_rs, oz_ss, oz_rs, uy_ss, uy_rs, uz_ss, uz_rs, ag_ss, ag_rs, pair_ss, pair_rs,
):
    width = left.shape[0]
    half = TILE // 2
    group, column = lax.axis_index("dp"), lax.axis_index("mp")
    z, plane = group // PLANES, group % PLANES
    other_plane = 1 - plane

    def ring(distance):
        return lax.rem(z + distance + RING, RING)

    up = (ring(1) * PLANES + plane, column)
    down = (ring(-1) * PLANES + plane, column)
    pair = (z * PLANES + other_plane, column)
    toward = (up, down)

    loads = [
        pltpu.make_async_copy(g_hbm.at[0], both.at[plane, :, pl.ds(0, width)], load_sem.at[0]),
        pltpu.make_async_copy(
            g_hbm.at[0, :, pl.ds(0, width // 2)], both.at[plane, :, pl.ds(width, width // 2)], load_sem.at[1]
        ),
        pltpu.make_async_copy(left_hbm.at[0], left, load_sem.at[2]),
        pltpu.make_async_copy(right_hbm.at[0], right, load_sem.at[3]),
    ]
    for load in loads:
        load.start()
    barrier = pltpu.get_barrier_semaphore()
    for neighbour in (up, down, pair):
        pl.semaphore_signal(barrier, inc=1, device_id=neighbour, device_id_type=pl.DeviceIdType.MESH)
    loads[0].wait()
    loads[1].wait()

    for row in range(width // TILE):
        turned = both[plane, row * TILE : (row + 1) * TILE, 0:width].T
        both[other_plane, :, row * TILE : (row + 1) * TILE] = turned
        if row < width // TILE // 2:
            both[other_plane, :, width + row * TILE : width + (row + 1) * TILE] = turned

    def statistic(slot):
        chunk = ring(DISTANCES[slot])
        rows = tile_at(chunk)
        columns = pl.ds(pl.multiple_of(chunk * TILE, TILE), PACKED)
        other[slot] = jnp.dot(both[1, rows, 0:width], both[0, :, columns], preferred_element_type=F32)
        mine[slot] = jnp.dot(both[0, rows, 0:width], both[1, :, columns], preferred_element_type=F32)

    streams = {
        "mz": (mine, mz_send, mz_recv, (mz_ss, mz_rs)),
        "oz": (other, oz_send, oz_recv, (oz_ss, oz_rs)),
        "uz": (lg, uz_send, uz_recv, (uz_ss, uz_rs)),
    }

    def ring_copy(name, step, way):
        own, send, recv, sems = streams[name]
        rows = own.shape[1]
        if step == 0:
            part = pl.ds(way * (rows // 2), rows // 2)
            return remote(send.at[0, 0, part], recv.at[0, 0, part], sems, (0, way), toward[way])
        return remote(send.at[step, way], recv.at[step, way], sems, (step, way), toward[way])

    def ring_step(name, step):
        own, send, recv, sems = streams[name]
        rows = own.shape[1]
        if step == 0:
            send[0, 0] = own[0].astype(BF16)
            for way in (UP, DOWN):
                ring_copy(name, 0, way).start()
            return
        for way in (UP, DOWN):
            slot = SLOT[(4 - step) * (1 if way == UP else -1)]
            ring_copy(name, step - 1, way).wait_recv()
            if step == 1:
                lo, hi = way * (rows // 2), (way + 1) * (rows // 2)
                rest_lo, rest_hi = (1 - way) * (rows // 2), (2 - way) * (rows // 2)
                send[1, way, lo:hi] = (own[slot, lo:hi] + recv[0, 0, lo:hi].astype(F32)).astype(BF16)
                send[1, way, rest_lo:rest_hi] = own[slot, rest_lo:rest_hi].astype(BF16)
            else:
                send[step, way] = (own[slot] + recv[step - 1, way].astype(F32)).astype(BF16)
            ring_copy(name, step, way).start()

    def ring_total(name):
        own, send, recv, sems = streams[name]
        ring_copy(name, 3, UP).wait_recv()
        ring_copy(name, 3, DOWN).wait_recv()
        return own[7] + recv[3, UP].astype(F32) + recv[3, DOWN].astype(F32)

    def update_copy(slot):
        return remote(uy_send.at[slot], uy_recv.at[slot], (uy_ss, uy_rs), slot, pair)

    def update_part(slot):
        rows = tile_at(ring(DISTANCES[slot]))
        lg_tmp[...] = jnp.dot(left[rows, :], both[plane, :, 0:width], preferred_element_type=F32)
        uy_send[slot] = lg_tmp[pl.ds(pl.multiple_of(other_plane * half, half), half), :].astype(BF16)
        update_copy(slot).start()
        lg[slot] = lg_tmp[pl.ds(pl.multiple_of(plane * half, half), half), :]

    def update_join(slot):
        update_copy(slot).wait_recv()
        lg[slot] = lg[slot] + uy_recv[slot].astype(F32)

    statistic(0)
    pl.semaphore_wait(barrier, 3)
    ring_step("oz", 0)
    ring_step("mz", 0)
    statistic(1)
    statistic(2)
    ring_step("oz", 1)
    ring_step("mz", 1)
    statistic(3)
    statistic(4)
    loads[2].wait()
    for slot in range(4):
        update_part(slot)
    ring_step("oz", 2)
    ring_step("mz", 2)
    statistic(5)
    statistic(6)
    statistic(7)
    for slot in range(4, 8):
        update_part(slot)
    ring_step("oz", 3)
    ring_step("mz", 3)
    swap = remote(swap_send, swap_recv, (pair_ss, pair_rs), 0, pair)
    swap_send[...] = ring_total("oz").astype(BF16)
    swap.start()
    mine[7] = ring_total("mz")
    update_join(0)
    ring_step("uz", 0)
    for slot in (1, 2):
        update_join(slot)
    ring_step("uz", 1)
    swap.wait_recv()
    packed[z] = (mine[7] + swap_recv[...].astype(F32)).astype(BF16)

    def gather_copy(step, way, part):
        chunk = ring(-step if way == UP else step)
        piece = packed.at[chunk, pl.ds(part * half, half)]
        return remote(piece, piece, (ag_ss, ag_rs), (step, way, part), toward[way])

    def gather_wait(step, way, part):
        chunk = ring(-step - 1 if way == UP else step + 1)
        piece = packed.at[chunk, pl.ds(part * half, half)]
        remote(piece, piece, (ag_ss, ag_rs), (step, way, part), toward[way]).wait_recv()

    def unpack(distance):
        chunk = ring(distance)
        for offset in range(5):
            block = packed[chunk, :, offset * TILE : (offset + 1) * TILE]
            place = lax.rem(chunk + offset, RING)
            full[tile_at(chunk), tile_at(place)] = block
            if offset in (1, 2, 3):
                full[tile_at(place), tile_at(chunk)] = block.T

    def gathers(step):
        return [(way, part) for part in (0, 1) for way in (UP, DOWN) if step < 3 or part == way]

    for way, part in gathers(0):
        gather_copy(0, way, part).start()
    unpack(0)
    for step in (1, 2, 3):
        for part in (0, 1):
            for way in (UP, DOWN):
                gather_wait(step - 1, way, part)
                if (way, part) in gathers(step):
                    gather_copy(step, way, part).start()
        unpack(-step)
        unpack(step)
    for slot in (3, 4):
        update_join(slot)
    ring_step("uz", 2)
    for way, part in gathers(3):
        gather_wait(3, way, part)
    unpack(4)

    eye = lax.broadcasted_iota(jnp.int32, (TILE, TILE), 0) == lax.broadcasted_iota(jnp.int32, (TILE, TILE), 1)
    diagonal = jnp.zeros((TILE, TILE), F32)
    for tile in range(width // TILE):
        at = slice(tile * TILE, (tile + 1) * TILE)
        diagonal = diagonal + jnp.where(eye, full[at, at].astype(F32), 0.0)
    trace = jnp.sum(jnp.sum(diagonal, axis=0, keepdims=True), axis=1, keepdims=True)
    mean = trace / width
    inverse = 0.25 / (2.0 * mean + EPS)
    for tile in range(width // TILE):
        at = slice(tile * TILE, (tile + 1) * TILE)
        full[at, at] = (full[at, at].astype(F32) - jnp.where(eye, mean, 0.0)).astype(BF16)
    c = (5.0 - DAMP) * 0.25 - mean * inverse
    c2 = c * c
    c3 = c2 * c
    c4 = c2 * c2
    coefficients = [
        1.25 * c - 1.25 * c4 * c + c3 * c3,
        -(1.25 - 6.25 * c4 + 6.0 * c4 * c),
        -12.5 * c3 + 15.0 * c4,
        12.5 * c2 - 20.0 * c3,
        -6.25 * c + 15.0 * c2,
        1.25 - 6.0 * c,
    ]
    own_rows = full[tile_at(z), :].astype(F32) * inverse
    value = own_rows
    for power in (5, 4, 3, 2, 1):
        value = (
            jnp.dot(value.astype(BF16), full[...], preferred_element_type=F32) * inverse
            + coefficients[power] * own_rows
        )
        if power == 3:
            for slot in (5, 6):
                update_join(slot)
            ring_step("uz", 3)
    on_diagonal = (
        lax.broadcasted_iota(jnp.int32, (TILE, width), 0) + z * TILE
        == lax.broadcasted_iota(jnp.int32, (TILE, width), 1)
    )
    root_rows[...] = (value + jnp.where(on_diagonal, coefficients[0], 0.0)).astype(BF16)
    own_half = pl.ds(pl.multiple_of(plane * half, half), half)
    other_half = pl.ds(pl.multiple_of(other_plane * half, half), half)
    send_root = remote(root_rows.at[other_half], root_recv, (pair_ss, pair_rs), 1, pair)
    send_root.start()
    roots_out[plane] = root_rows[own_half, :]

    update_join(7)
    loads[3].wait()
    update_out[...] = jnp.dot(
        ring_total("uz").astype(BF16), right[...], preferred_element_type=F32
    ) / (RING * PLANES)
    send_root.wait_recv()
    roots_out[other_plane] = root_recv[...]

    for name in streams:
        for step in range(4):
            for way in (UP, DOWN):
                ring_copy(name, step, way).wait_send()
    for slot in range(8):
        update_copy(slot).wait_send()
    for step in range(4):
        for way, part in gathers(step):
            gather_copy(step, way, part).wait_send()
    swap.wait_send()
    send_root.wait_send()


def fused(grad_parts, stale_left, stale_right):
    width = grad_parts.shape[1]
    half = TILE // 2
    hbm = pl.BlockSpec(memory_space=pl.ANY)
    vmem = pl.BlockSpec(memory_space=pltpu.VMEM)
    dma = pltpu.SemaphoreType.DMA
    return pl.pallas_call(
        kernel,
        out_shape=(
            jax.ShapeDtypeStruct((half, width), F32),
            jax.ShapeDtypeStruct((PLANES, half, width), BF16),
        ),
        in_specs=[hbm] * 3,
        out_specs=(vmem, vmem),
        scratch_shapes=[
            pltpu.VMEM((2, width, width + width // 2), BF16),
            pltpu.VMEM((width, width), BF16),
            pltpu.VMEM((width, width), BF16),
            pltpu.VMEM((RING, TILE, PACKED), F32),
            pltpu.VMEM((RING, TILE, PACKED), F32),
            pltpu.VMEM((RING, half, width), F32),
            pltpu.VMEM((TILE, width), F32),
            pltpu.VMEM((4, 2, TILE, PACKED), BF16),
            pltpu.VMEM((4, 2, TILE, PACKED), BF16),
            pltpu.VMEM((4, 2, TILE, PACKED), BF16),
            pltpu.VMEM((4, 2, TILE, PACKED), BF16),
            pltpu.VMEM((RING, half, width), BF16),
            pltpu.VMEM((RING, half, width), BF16),
            pltpu.VMEM((4, 2, half, width), BF16),
            pltpu.VMEM((4, 2, half, width), BF16),
            pltpu.VMEM((TILE, PACKED), BF16),
            pltpu.VMEM((TILE, PACKED), BF16),
            pltpu.VMEM((RING, TILE, PACKED), BF16),
            pltpu.VMEM((width, width), BF16),
            pltpu.VMEM((TILE, width), BF16),
            pltpu.VMEM((half, width), BF16),
            dma((4,)),
            dma((4, 2)), dma((4, 2)), dma((4, 2)), dma((4, 2)),
            dma((RING,)), dma((RING,)),
            dma((4, 2)), dma((4, 2)),
            dma((4, 2, 2)), dma((4, 2, 2)),
            dma((2,)), dma((2,)),
        ],
        compiler_params=pltpu.CompilerParams(
            collective_id=0, has_side_effects=True, vmem_limit_bytes=52 << 20
        ),
        name="shampoo",
    )(grad_parts, stale_left, stale_right)


def per_device(grad_parts, params, stale_left, stale_right, step_matrix):
    rows = params.shape[0]
    row_at = lax.axis_index("dp") * rows
    owner = lax.axis_index("mp")
    update, roots = fused(grad_parts, stale_left, stale_right)

    def refreshed(side, stale):
        hit = jnp.any(step_matrix == 2 * owner + side)
        stale_rows = lax.dynamic_slice_in_dim(stale[0], row_at, rows, 0)
        return jnp.where(hit, roots[side], stale_rows)[None]

    new_params = params.astype(F32) - STEP_SIZE * update
    return (new_params, refreshed(0, stale_left), refreshed(1, stale_right))


def solution(mesh):
    return jax.shard_map(
        per_device,
        mesh=mesh,
        in_specs=(
            P("dp", None, "mp"),
            P("dp", "mp"),
            P("mp", None, None),
            P("mp", None, None),
            P(),
        ),
        out_specs=(P("dp", "mp"), P("mp", "dp", None), P("mp", "dp", None)),
        check_vma=False,
    )
```

time: 826 us -> 77.5 us (0.09)
  waiting for transfers between devices: 692 us -> 0 us
  Pallas kernels: 0 us -> 71.6 us
  blocking collectives: 42.7 us -> 0 us
  matrix products: 36.8 us -> 0 us
  local copies, waits for them, and re-layouts: 18.9 us -> 0.01 us
  between operations: 17.5 us -> 0.65 us
  other arithmetic: 13.9 us -> 5.09 us
    all_gather x4 -> x0, waiting for transfers between devices: 260 us -> none  [the longest x2 175 us: per_device(): everyone = lax.all_gather(factor, 'dp', axis=1, tiled=True)]
    reduce_scatter x1 -> x0, waiting for transfers between devices: 226 us -> none  [per_device(): lax.psum_scatter(jnp.concatenate([left_part, right_part], axis=1), 'dp',...]
    unnamed x7 -> x0, waiting for transfers between devices: 206 us -> none
    pallas_call x0 -> x1, Pallas kernels: none -> 71.6 us  [fused(): pl.pallas_call(kernel, out_shape=(jax.ShapeDtypeStruct((half, width), F32...]
    psum x1 -> x0, blocking collectives: 42.7 us -> none  [per_device(): total = lax.psum(diag_part, 'dp')]
    dot_general x9 -> x0, matrix products: 36.8 us -> none  [the longest x6 23.4 us: batched(): jnp.einsum('sij,sjk->sik', left, right, precision=HIGH, preferred_element...]
    unnamed x13 -> x2, local copies, waits for them, and re-layouts: 18.3 us -> 0.01 us
  transfers between devices with their start and end apart: 6 -> 0, of which waited for: 6 -> 0; matrix products, arithmetic and copies ran while one was open for 3% -> 0% of each run, Pallas kernels for 0% -> 0%
where the time goes in v1:
time: 77.5 us; the launch traced here: 77.4 us
  Pallas kernels  71.6 us (92%)
  other arithmetic  5.09 us (7%)
    pallas_call x1, Pallas kernels, fused(): pl.pallas_call(kernel, out_shape=(jax.ShapeDtypeStruct((half, width), F32...  71.6 us
    select_n x1, other arithmetic, refreshed(): return jnp.where(hit, roots[side], stale_rows)[None]  2.98 us

profile of v1, /device:TPU:6, one launch (start us, length us, event | category | flops | bytes accessed | tf_op | source)
XLA Modules:
  0.0 77.4 jit_solution(14726534841350378245)
XLA Ops:
  0.6 1.4 %compare_reduce_fusion = (pred[]{:T(512)}, pred[]{:T(512)}) fusion(s32[16]{0:T(128)} %param.9, s32[]{:T(128)S(6)} %add.8, s32[]{:T(128)S(6)} %mul.15), kind=kLoop, calls=%fused_computation.3 | loop fusion | flops 62 | bytes 74 | tf_op jit(solution)/shard_map/reduce_or | solution.py:340
  2.0 0.0 copy-start
  2.0 71.6 %shampoo.1 = (f32[64,1024]{1,0:T(8,128)S(1)}, bf16[2,64,1024]{2,1,0:T(8,128)(2,1)S(1)}) custom-call(bf16[1,1024,1024]{2,1,0:T(8,128)(2,1)} %g_hbm.1, bf16[1,1024,1024]{2,1,0:T(8,128)(2,1)} %left_hbm.1, bf16[1,1024,1024]{2,1,0:T(8,128)(2,1)} %right_hbm.1), custom_call_target="tpu_custom_call" | custom-call | tf_op jit(solution)/shard_map/shampoo/pallas_call | solution.py:289
  73.7 0.0 copy-done
  73.7 0.7 multiply_subtract_fusion
  74.4 3.0 %dynamic-slice_select_fusion = (bf16[1,64,1024]{2,1,0:T(8,128)(2,1)}, bf16[1,64,1024]{2,1,0:T(8,128)(2,1)}) fusion(bf16[1,1024,1024]{2,1,0:T(8,128)(2,1)} %right_hbm.1, s32[]{:T(128)S(6)} %select_n.21, bf16[2,64,1024]{2,1,0:T(8,128)(2,1)S(1)} %get-tuple-element.6, pred[]{:T(512)} %get-tuple-element.7, bf16[1,1024,1024]{2,1,0:T(8,128)(2,1)} %left_hbm.1, ...), kind=kLoop, calls=%fused_computation.1 | loop fusion | flops 131072 | bytes 786438 | tf_op jit(solution)/shard_map/jit(_where)/select_n | solution.py:342
Async XLA Ops:
  2.0 71.7 %copy-start = (bf16[64,1024]{1,0:T(8,128)(2,1)S(1)}, bf16[64,1024]{1,0:T(8,128)(2,1)}, u32[]{:S(2)}) copy-start(bf16[64,1024]{1,0:T(8,128)(2,1)} %param.6) | copy-start | bytes 393220

commit v2 on v0

v2 whole, which is shorter than its diff:
```python
import jax
import jax.numpy as jnp
from jax import lax
from jax.experimental import pallas as pl
from jax.experimental.pallas import tpu as pltpu
from jax.sharding import PartitionSpec as P

EPS = 1e-06
DAMP = 0.05
STEP_SIZE = 0.5
RING = 8
PLANES = 2
TILE = 128
PACKED = 4 * TILE
RING_FIRST = 3 * TILE
PLANE_ROWS = PACKED - RING_FIRST + TILE // 2
DISTANCES = (4, 3, -3, 2, -2, 1, -1, 0)
SLOT = {distance: slot for slot, distance in enumerate(DISTANCES)}
F32 = jnp.float32
BF16 = jnp.bfloat16
UP, DOWN = 0, 1


SCHEDULE = (
    ("others", 0),
    ("ring_step", "oz", 0),
    ("mines", 0),
    ("ring_step", "mz", 0),
    ("statistic", 1),
    ("statistic", 2),
    ("join", 0),
    ("ring_step", "my", 0),
    ("statistic", 3),
    ("statistic", 4),
    ("ring_step", "oz", 1),
    ("ring_step", "mz", 1),
    ("statistic", 5),
    ("statistic", 6),
    ("statistic", 7),
    ("join", 1),
    ("join", 2),
    ("ring_step", "my", 1),
    ("ring_step", "oz", 2),
    ("ring_step", "mz", 2),
    ("load_wait", 2),
    ("update_part", 0),
    ("update_part", 1),
    ("update_part", 2),
    ("update_part", 3),
    ("join", 3),
    ("join", 4),
    ("ring_step", "my", 2),
    ("ring_step", "oz", 3),
    ("ring_step", "mz", 3),
    ("join", 5),
    ("join", 6),
    ("ring_step", "my", 3),
    ("update_join", 0),
    ("ring_step", "uz", 0),
    ("swap_start",),
    ("update_part", 4),
    ("update_part", 5),
    ("update_part", 6),
    ("update_part", 7),
    ("join", 7),
    ("total_y",),
    ("gather_step", 0, 0),
    ("total_z",),
    ("update_join", 1),
    ("update_join", 2),
    ("swap_done",),
    ("gather_step", 1, 0),
    ("ring_step", "uz", 1),
    ("unpack", 0, 0),
    ("unpack", 1, 0),
    ("gather_step", 0, 1),
    ("unpack", 0, 1, -1),
    ("gather_step", 1, 1),
    ("unpack", 1, 1, -1),
    ("gather_step", 0, 2),
    ("unpack", 0, 2, -2),
    ("gather_step", 1, 2),
    ("unpack", 1, 2, -2),
    ("gather_step", 0, 3),
    ("unpack", 0, 3, -3),
    ("gather_step", 1, 3),
    ("unpack", 1, 3, -3),
    ("update_join", 3),
    ("update_join", 4),
    ("ring_step", "uz", 2),
    ("gather_done", 0),
    ("unpack", 0, 4),
    ("unpack_far", 0, 1, 2, 3),
    ("gather_done", 1),
    ("unpack", 1, 4),
    ("center",),
    ("newton", 5, 4, 3),
    ("update_join", 5),
    ("update_join", 6),
    ("ring_step", "uz", 3),
    ("newton", 2, 1),
    ("root_send",),
    ("update_join", 7),
    ("load_wait", 3),
    ("load_wait", 4),
    ("update_final",),
    ("roots_final",),
)


def remote(src, dst, sems, at, device):
    return pltpu.make_async_remote_copy(
        src_ref=src,
        dst_ref=dst,
        send_sem=sems[0].at[at],
        recv_sem=sems[1].at[at],
        device_id=device,
        device_id_type=pl.DeviceIdType.MESH,
    )


def tile_at(index):
    return pl.ds(pl.multiple_of(index * TILE, TILE), TILE)


def kernel(
    step_hbm, g_hbm, left_hbm, right_hbm, update_out, left_out, right_out,
    both, left, right, mz, oz, my, lg, lg_tmp,
    mz_send, mz_recv, oz_send, oz_recv, my_send, my_recv, uz_send, uz_recv,
    sy_send, sy_recv, uy_send, uy_recv,
    swap_send, swap_recv, packed_z, packed_y, full, root_rows, root_recv, roots,
    step_ref, load_sem, mz_ss, mz_rs, oz_ss, oz_rs, my_ss, my_rs, uz_ss, uz_rs,
    sy_ss, sy_rs, uy_ss, uy_rs, ag_ss, ag_rs, pair_ss, pair_rs,
):
    width = left.shape[0]
    half = TILE // 2
    group, column = lax.axis_index("dp"), lax.axis_index("mp")
    z, plane = group // PLANES, group % PLANES
    other_plane = 1 - plane

    def ring(distance):
        return lax.rem(z + distance + RING, RING)

    up = (ring(1) * PLANES + plane, column)
    down = (ring(-1) * PLANES + plane, column)
    pair = (z * PLANES + other_plane, column)
    toward = (up, down)
    own_half = pl.ds(pl.multiple_of(plane * half, half), half)
    other_half = pl.ds(pl.multiple_of(other_plane * half, half), half)

    started, waiting = [], {}

    def start(key, copy):
        copy.start()
        started.append(copy)
        waiting[key] = copy

    def received(key, copy):
        copy.wait_recv()
        del waiting[key]

    barrier = pltpu.get_barrier_semaphore()
    for neighbour in (up, down, pair):
        pl.semaphore_signal(barrier, inc=1, device_id=neighbour, device_id_type=pl.DeviceIdType.MESH)
    loads = [
        pltpu.make_async_copy(g_hbm.at[0], both.at[plane, :, pl.ds(0, width)], load_sem.at[0]),
        pltpu.make_async_copy(
            g_hbm.at[0, :, pl.ds(0, PACKED - TILE)], both.at[plane, :, pl.ds(width, PACKED - TILE)], load_sem.at[1]
        ),
        pltpu.make_async_copy(left_hbm.at[0], left, load_sem.at[2]),
        pltpu.make_async_copy(right_hbm.at[0], right, load_sem.at[3]),
        pltpu.make_async_copy(step_hbm, step_ref, load_sem.at[4]),
    ]
    loads[0].start()
    loads[1].start()
    loads[0].wait()
    loads[1].wait()
    for load in loads[2:]:
        load.start()

    for row in range(width // TILE):
        turned = both[plane, row * TILE : (row + 1) * TILE, 0:width].T
        both[other_plane, :, row * TILE : (row + 1) * TILE] = turned
        if row < PACKED // TILE - 1:
            both[other_plane, :, width + row * TILE : width + (row + 1) * TILE] = turned

    def plane_copy(slot):
        return remote(sy_send.at[slot], sy_recv.at[slot], (sy_ss, sy_rs), slot, pair)

    def product(slot, first, second, whole, pieces):
        chunk = ring(DISTANCES[slot])
        rows = tile_at(chunk)
        columns = pl.ds(pl.multiple_of(chunk * TILE, TILE), PACKED)
        tiles = jnp.dot(both[first, rows, 0:width], both[second, :, columns], preferred_element_type=F32)
        whole[slot] = tiles[:, :RING_FIRST]
        for at in range(RING_FIRST, PACKED, TILE):
            pieces[slot, at - RING_FIRST : at - RING_FIRST + TILE] = tiles[:, at : at + TILE].astype(pieces.dtype)
        upper = chunk // 4
        rows = pl.ds(pl.multiple_of((chunk - 4 * upper) * TILE + upper * half, half), half)
        columns = tile_at(chunk - 4 * upper + 4)
        tile = jnp.dot(both[first, rows, 0:width], both[second, :, columns], preferred_element_type=F32)
        pieces[slot, PLANE_ROWS - half :] = tile.astype(pieces.dtype)

    def others(*slots):
        for slot in slots:
            product(slot, 1, 0, oz, sy_send)
            start(("sy", slot), plane_copy(slot))

    def mines(*slots):
        for slot in slots:
            product(slot, 0, 1, mz, my)

    def statistic(*slots):
        for slot in slots:
            others(slot)
            mines(slot)

    def join(*slots):
        for slot in slots:
            received(("sy", slot), plane_copy(slot))
            my[slot] = my[slot] + sy_recv[slot].astype(F32)

    streams = {
        "mz": (mz, mz_send, mz_recv, (mz_ss, mz_rs)),
        "oz": (oz, oz_send, oz_recv, (oz_ss, oz_rs)),
        "my": (my, my_send, my_recv, (my_ss, my_rs)),
        "uz": (lg, uz_send, uz_recv, (uz_ss, uz_rs)),
    }

    def ring_copy(name, step, way):
        own, send, recv, sems = streams[name]
        rows = own.shape[1]
        if step == 0:
            part = pl.ds(way * (rows // 2), rows // 2)
            return remote(send.at[0, 0, part], recv.at[0, 0, part], sems, (0, way), toward[way])
        return remote(send.at[step, way], recv.at[step, way], sems, (step, way), toward[way])

    def ring_step(name, step):
        own, send, recv, sems = streams[name]
        rows = own.shape[1]
        if step == 0:
            send[0, 0] = own[0].astype(BF16)
            for way in (UP, DOWN):
                start((name, 0, way), ring_copy(name, 0, way))
            return
        for way in (UP, DOWN):
            slot = SLOT[(4 - step) * (1 if way == UP else -1)]
            received((name, step - 1, way), ring_copy(name, step - 1, way))
            if step == 1:
                lo, hi = way * (rows // 2), (way + 1) * (rows // 2)
                rest_lo, rest_hi = (1 - way) * (rows // 2), (2 - way) * (rows // 2)
                send[1, way, lo:hi] = (own[slot, lo:hi] + recv[0, 0, lo:hi].astype(F32)).astype(BF16)
                send[1, way, rest_lo:rest_hi] = own[slot, rest_lo:rest_hi].astype(BF16)
            else:
                send[step, way] = (own[slot] + recv[step - 1, way].astype(F32)).astype(BF16)
            start((name, step, way), ring_copy(name, step, way))

    def ring_total(name):
        own, send, recv, sems = streams[name]
        received((name, 3, UP), ring_copy(name, 3, UP))
        received((name, 3, DOWN), ring_copy(name, 3, DOWN))
        return own[7] + recv[3, UP].astype(F32) + recv[3, DOWN].astype(F32)

    def update_copy(slot):
        return remote(uy_send.at[slot], uy_recv.at[slot], (uy_ss, uy_rs), slot, pair)

    def update_part(*slots):
        for slot in slots:
            rows = tile_at(ring(DISTANCES[slot]))
            lg_tmp[...] = jnp.dot(left[rows, :], both[plane, :, 0:width], preferred_element_type=F32)
            uy_send[slot] = lg_tmp[other_half, :].astype(BF16)
            start(("uy", slot), update_copy(slot))
            lg[slot] = lg_tmp[own_half, :]

    def update_join(*slots):
        for slot in slots:
            received(("uy", slot), update_copy(slot))
            lg[slot] = lg[slot] + uy_recv[slot].astype(F32)

    parts = (packed_y, packed_z)

    def gather_copy(part, step, way):
        piece = parts[part].at[ring(-step if way == UP else step)]
        return remote(piece, piece, (ag_ss, ag_rs), (part, step, way), toward[way])

    def gather_wait(part, step, way):
        piece = parts[part].at[ring(-step - 1 if way == UP else step + 1)]
        received(("ag", part, step, way), remote(piece, piece, (ag_ss, ag_rs), (part, step, way), toward[way]))

    def gather_ways(part, step):
        return (UP, DOWN) if step < 3 else (part,)

    def gather_step(part, step):
        for way in (UP, DOWN):
            if step > 0:
                gather_wait(part, step - 1, way)
            if way in gather_ways(part, step):
                start(("ag", part, step, way), gather_copy(part, step, way))

    def place(rows, columns, block, turned):
        full[rows, columns] = block
        if turned:
            full[columns, rows] = block.T

    def unpack(part, *distances):
        for distance in distances:
            chunk = ring(distance)
            for offset in range(PACKED // TILE):
                at = offset * TILE
                if (at < RING_FIRST) == (part == 1):
                    block = (
                        packed_z[chunk, :, at : at + TILE]
                        if part == 1
                        else packed_y[chunk, at - RING_FIRST : at - RING_FIRST + TILE]
                    )
                    place(tile_at(chunk), tile_at(lax.rem(chunk + offset, RING)), block, offset > 0)

    def unpack_far(*distances):
        for distance in distances:
            lower = lax.rem(ring(distance), 4)
            block = jnp.concatenate(
                [packed_y[lower, PLANE_ROWS - half :], packed_y[lower + 4, PLANE_ROWS - half :]], axis=0
            )
            place(tile_at(lower), tile_at(lower + 4), block, True)

    def load_wait(*which):
        for index in which:
            loads[index].wait()

    def swap_copy():
        return remote(swap_send, swap_recv, (pair_ss, pair_rs), 0, pair)

    def swap_start():
        swap_send[...] = ring_total("oz").astype(BF16)
        start("swap", swap_copy())

    def total_y():
        packed_y[z] = ring_total("my").astype(BF16)

    def total_z():
        mz[7] = ring_total("mz")

    def swap_done():
        received("swap", swap_copy())
        packed_z[z] = (mz[7] + swap_recv[...].astype(F32)).astype(BF16)

    def gather_done(part):
        for way in gather_ways(part, 3):
            gather_wait(part, 3, way)

    state = {}

    def center():
        eye = lax.broadcasted_iota(jnp.int32, (TILE, TILE), 0) == lax.broadcasted_iota(jnp.int32, (TILE, TILE), 1)
        tiles = [slice(at, at + TILE) for at in range(0, width, TILE)]
        diagonal = jnp.zeros((TILE, TILE), F32)
        for at in tiles:
            diagonal = diagonal + jnp.where(eye, full[at, at].astype(F32), 0.0)
        trace = jnp.sum(jnp.sum(diagonal, axis=0, keepdims=True), axis=1, keepdims=True)
        mean = trace / width
        inverse = 0.25 / (2.0 * mean + EPS)
        for at in tiles:
            full[at, at] = (full[at, at].astype(F32) - jnp.where(eye, mean, 0.0)).astype(BF16)
        c = (5.0 - DAMP) * 0.25 - mean * inverse
        c2 = c * c
        c3 = c2 * c
        c4 = c2 * c2
        state["coefficients"] = [
            1.25 * c - 1.25 * c4 * c + c3 * c3,
            -(1.25 - 6.25 * c4 + 6.0 * c4 * c),
            -12.5 * c3 + 15.0 * c4,
            12.5 * c2 - 20.0 * c3,
            -6.25 * c + 15.0 * c2,
            1.25 - 6.0 * c,
        ]
        state["inverse"] = inverse
        state["rows"] = state["value"] = full[tile_at(z), :].astype(F32) * inverse

    def newton(*powers):
        for power in powers:
            state["value"] = (
                jnp.dot(state["value"].astype(BF16), full[...], preferred_element_type=F32) * state["inverse"]
                + state["coefficients"][power] * state["rows"]
            )

    def root_copy():
        return remote(root_rows.at[other_half], root_recv, (pair_ss, pair_rs), 1, pair)

    def root_send():
        on_diagonal = (
            lax.broadcasted_iota(jnp.int32, (TILE, width), 0) + z * TILE
            == lax.broadcasted_iota(jnp.int32, (TILE, width), 1)
        )
        root_rows[...] = (state["value"] + jnp.where(on_diagonal, state["coefficients"][0], 0.0)).astype(BF16)
        start("root", root_copy())
        roots[plane] = root_rows[own_half, :]

    def update_final():
        total = ring_total("uz").astype(BF16)
        update_out[...] = jnp.dot(total, right[...], preferred_element_type=F32) / (RING * PLANES)

    def roots_final():
        received("root", root_copy())
        roots[other_plane] = root_recv[...]
        own_at = pl.ds(pl.multiple_of(group * half, half), half)
        for side, stale, out in ((0, left, left_out), (1, right, right_out)):
            hits = jnp.int32(0)
            for owner in range(step_ref.shape[0]):
                hits = hits + (step_ref[owner] == 2 * column + side).astype(jnp.int32)
            out[0] = jnp.where(jnp.full((half, width), hits) > 0, roots[side], stale[own_at, :])

    pl.semaphore_wait(barrier, 3)
    operations = {
        operation.__name__: operation
        for operation in (
            others, mines, statistic, join, ring_step, load_wait, update_part, update_join, swap_start, swap_done,
            total_y, total_z, gather_step, gather_done, unpack, unpack_far, center, newton, root_send,
            update_final, roots_final,
        )
    }
    for name, *values in SCHEDULE:
        operations[name](*values)

    for copy in started:
        copy.wait_send()


def per_device(grad_parts, params, stale_left, stale_right, step_matrix):
    width = grad_parts.shape[1]
    half = TILE // 2
    hbm = pl.BlockSpec(memory_space=pltpu.HBM)
    vmem = pl.BlockSpec(memory_space=pltpu.VMEM)
    dma = pltpu.SemaphoreType.DMA

    def ring_buffers(rows, columns):
        return [pltpu.VMEM((4, 2, rows, columns), BF16)] * 2

    update, left_roots, right_roots = pl.pallas_call(
        kernel,
        out_shape=(
            jax.ShapeDtypeStruct((half, width), F32),
            jax.ShapeDtypeStruct((1, half, width), BF16),
            jax.ShapeDtypeStruct((1, half, width), BF16),
        ),
        in_specs=[hbm] * 4,
        out_specs=(vmem, vmem, vmem),
        scratch_shapes=[
            pltpu.VMEM((2, width, width + PACKED - TILE), BF16),
            pltpu.VMEM((width, width), BF16),
            pltpu.VMEM((width, width), BF16),
            pltpu.VMEM((RING, TILE, RING_FIRST), F32),
            pltpu.VMEM((RING, TILE, RING_FIRST), F32),
            pltpu.VMEM((RING, PLANE_ROWS, TILE), F32),
            pltpu.VMEM((RING, half, width), F32),
            pltpu.VMEM((TILE, width), F32),
            *ring_buffers(TILE, RING_FIRST),
            *ring_buffers(TILE, RING_FIRST),
            *ring_buffers(PLANE_ROWS, TILE),
            *ring_buffers(half, width),
            pltpu.VMEM((RING, PLANE_ROWS, TILE), BF16),
            pltpu.VMEM((RING, PLANE_ROWS, TILE), BF16),
            pltpu.VMEM((RING, half, width), BF16),
            pltpu.VMEM((RING, half, width), BF16),
            pltpu.VMEM((TILE, RING_FIRST), BF16),
            pltpu.VMEM((TILE, RING_FIRST), BF16),
            pltpu.VMEM((RING, TILE, RING_FIRST), BF16),
            pltpu.VMEM((RING, PLANE_ROWS, TILE), BF16),
            pltpu.VMEM((width, width), BF16),
            pltpu.VMEM((TILE, width), BF16),
            pltpu.VMEM((half, width), BF16),
            pltpu.VMEM((2, half, width), BF16),
            pltpu.SMEM((16,), jnp.int32),
            dma((5,)),
            *[dma((4, 2))] * 8,
            *[dma((RING,))] * 4,
            *[dma((2, 4, 2))] * 2,
            *[dma((2,))] * 2,
        ],
        compiler_params=pltpu.CompilerParams(
            collective_id=0, has_side_effects=True, vmem_limit_bytes=52 << 20
        ),
        name="shampoo",
    )(step_matrix, grad_parts, stale_left, stale_right)
    return params.astype(F32) - STEP_SIZE * update, left_roots, right_roots


def solution(mesh):
    return jax.shard_map(
        per_device,
        mesh=mesh,
        in_specs=(
            P("dp", None, "mp"),
            P("dp", "mp"),
            P("mp", None, None),
            P("mp", None, None),
            P(),
        ),
        out_specs=(P("dp", "mp"), P("mp", "dp", None), P("mp", "dp", None)),
        check_vma=False,
    )
```

time: 826 us -> 67.5 us (0.08)
  waiting for transfers between devices: 692 us -> 0 us
  Pallas kernels: 0 us -> 64.1 us
  blocking collectives: 42.7 us -> 0 us
  matrix products: 36.8 us -> 0 us
  local copies, waits for them, and re-layouts: 18.9 us -> 1.96 us
  between operations: 17.5 us -> 0.66 us
  other arithmetic: 13.9 us -> 0.73 us
    all_gather x4 -> x0, waiting for transfers between devices: 260 us -> none  [the longest x2 175 us: per_device(): everyone = lax.all_gather(factor, 'dp', axis=1, tiled=True)]
    reduce_scatter x1 -> x0, waiting for transfers between devices: 226 us -> none  [per_device(): lax.psum_scatter(jnp.concatenate([left_part, right_part], axis=1), 'dp',...]
    unnamed x7 -> x0, waiting for transfers between devices: 206 us -> none
    pallas_call x0 -> x1, Pallas kernels: none -> 64.1 us  [per_device(): pl.pallas_call(kernel, out_shape=(jax.ShapeDtypeStruct((half, width), F32...]
    psum x1 -> x0, blocking collectives: 42.7 us -> none  [per_device(): total = lax.psum(diag_part, 'dp')]
    dot_general x9 -> x0, matrix products: 36.8 us -> none  [the longest x6 23.4 us: batched(): jnp.einsum('sij,sjk->sik', left, right, precision=HIGH, preferred_element...]
    unnamed x13 -> x6, local copies, waits for them, and re-layouts: 18.3 us -> 1.96 us
  transfers between devices with their start and end apart: 6 -> 0, of which waited for: 6 -> 0; matrix products, arithmetic and copies ran while one was open for 3% -> 0% of each run, Pallas kernels for 0% -> 0%
where the time goes in v2:
time: 67.5 us; the launch traced here: 67.4 us
  Pallas kernels  64.1 us (95%)
  local copies, waits for them, and re-layouts  1.96 us (3%)
  other arithmetic  0.73 us (1%)
    pallas_call x1, Pallas kernels, per_device(): pl.pallas_call(kernel, out_shape=(jax.ShapeDtypeStruct((half, width), F32...  64.1 us
    unnamed x6, local copies, waits for them, and re-layouts  1.96 us

profile of v2, /device:TPU:6, one launch (start us, length us, event | category | flops | bytes accessed | tf_op | source)
XLA Modules:
  0.0 67.4 jit_solution(15592188134324586005)
XLA Ops:
  0.6 0.0 copy-start
  0.6 0.6 copy-done
  1.3 0.0 copy-start.1
  1.3 64.1 %shampoo.1 = (f32[64,1024]{1,0:T(8,128)S(1)}, bf16[1,64,1024]{2,1,0:T(8,128)(2,1)S(1)}, bf16[1,64,1024]{2,1,0:T(8,128)(2,1)S(1)}) custom-call(s32[16]{0:T(128)S(1)} %copy-done, bf16[1,1024,1024]{2,1,0:T(8,128)(2,1)} %g_hbm.1, bf16[1,1024,1024]{2,1,0:T(8,128)(2,1)} %left_hbm.1, bf16[1,1024,1024]{2,1,0:T(8,128)(2,1)} %right_hbm.1), custom_call_target="tpu_custom_call" | custom-call | tf_op jit(solution)/shard_map/shampoo/pallas_call | solution.py:438
  65.4 0.0 copy-done.1
  65.4 0.7 %multiply_subtract_fusion = f32[64,1024]{1,0:T(8,128)} fusion(f32[64,1024]{1,0:T(8,128)S(1)} %get-tuple-element.6, bf16[64,1024]{1,0:T(8,128)(2,1)S(1)} %copy-done.1), kind=kLoop, calls=%fused_computation | loop fusion | flops 196608 | bytes 655360 | tf_op jit(solution)/shard_map/sub | solution.py:484
  66.1 0.7 copy.10
  66.8 0.7 copy.11
Async XLA Ops:
  0.6 0.7 copy-start
  1.3 64.1 %copy-start.1 = (bf16[64,1024]{1,0:T(8,128)(2,1)S(1)}, bf16[64,1024]{1,0:T(8,128)(2,1)}, u32[]{:S(2)}) copy-start(bf16[64,1024]{1,0:T(8,128)(2,1)} %param.6) | copy-start | bytes 393220

commit v3 on v2

--- a/solution.py
+++ b/solution.py
@@ -12,7 +12,7 @@
 PLANES = 2
 TILE = 128
 PACKED = 4 * TILE
-RING_FIRST = 3 * TILE
+RING_FIRST = 2 * TILE
 PLANE_ROWS = PACKED - RING_FIRST + TILE // 2
 DISTANCES = (4, 3, -3, 2, -2, 1, -1, 0)
 SLOT = {distance: slot for slot, distance in enumerate(DISTANCES)}
@@ -21,91 +21,7 @@
 UP, DOWN = 0, 1
 
 
-SCHEDULE = (
-    ("others", 0),
-    ("ring_step", "oz", 0),
-    ("mines", 0),
-    ("ring_step", "mz", 0),
-    ("statistic", 1),
-    ("statistic", 2),
-    ("join", 0),
-    ("ring_step", "my", 0),
-    ("statistic", 3),
-    ("statistic", 4),
-    ("ring_step", "oz", 1),
-    ("ring_step", "mz", 1),
-    ("statistic", 5),
-    ("statistic", 6),
-    ("statistic", 7),
-    ("join", 1),
-    ("join", 2),
-    ("ring_step", "my", 1),
-    ("ring_step", "oz", 2),
-    ("ring_step", "mz", 2),
-    ("load_wait", 2),
-    ("update_part", 0),
-    ("update_part", 1),
-    ("update_part", 2),
-    ("update_part", 3),
-    ("join", 3),
-    ("join", 4),
-    ("ring_step", "my", 2),
-    ("ring_step", "oz", 3),
-    ("ring_step", "mz", 3),
-    ("join", 5),
-    ("join", 6),
-    ("ring_step", "my", 3),
-    ("update_join", 0),
-    ("ring_step", "uz", 0),
-    ("swap_start",),
-    ("update_part", 4),
-    ("update_part", 5),
-    ("update_part", 6),
-    ("update_part", 7),
-    ("join", 7),
-    ("total_y",),
-    ("gather_step", 0, 0),
-    ("total_z",),
-    ("update_join", 1),
-    ("update_join", 2),
-    ("swap_done",),
-    ("gather_step", 1, 0),
-    ("ring_step", "uz", 1),
-    ("unpack", 0, 0),
-    ("unpack", 1, 0),
-    ("gather_step", 0, 1),
-    ("unpack", 0, 1, -1),
-    ("gather_step", 1, 1),
-    ("unpack", 1, 1, -1),
-    ("gather_step", 0, 2),
-    ("unpack", 0, 2, -2),
-    ("gather_step", 1, 2),
-    ("unpack", 1, 2, -2),
-    ("gather_step", 0, 3),
-    ("unpack", 0, 3, -3),
-    ("gather_step", 1, 3),
-    ("unpack", 1, 3, -3),
-    ("update_join", 3),
-    ("update_join", 4),
-    ("ring_step", "uz", 2),
-    ("gather_done", 0),
-    ("unpack", 0, 4),
-    ("unpack_far", 0, 1, 2, 3),
-    ("gather_done", 1),
-    ("unpack", 1, 4),
-    ("center",),
-    ("newton", 5, 4, 3),
-    ("update_join", 5),
-    ("update_join", 6),
-    ("ring_step", "uz", 3),
-    ("newton", 2, 1),
-    ("root_send",),
-    ("update_join", 7),
-    ("load_wait", 3),
-    ("load_wait", 4),
-    ("update_final",),
-    ("roots_final",),
-)
+OZ, MZ, MY, UZ = range(4)
 
 
 def remote(src, dst, sems, at, device):
@@ -124,7 +40,7 @@
 
 
 def kernel(
-    step_hbm, g_hbm, left_hbm, right_hbm, update_out, left_out, right_out,
+    step_hbm, g_hbm, left_hbm, right_hbm, update_out, roots_out,
     both, left, right, mz, oz, my, lg, lg_tmp,
     mz_send, mz_recv, oz_send, oz_recv, my_send, my_recv, uz_send, uz_recv,
     sy_send, sy_recv, uy_send, uy_recv,
@@ -210,22 +126,17 @@
         for slot in slots:
             product(slot, 0, 1, mz, my)
 
-    def statistic(*slots):
-        for slot in slots:
-            others(slot)
-            mines(slot)
-
     def join(*slots):
         for slot in slots:
             received(("sy", slot), plane_copy(slot))
             my[slot] = my[slot] + sy_recv[slot].astype(F32)
 
-    streams = {
-        "mz": (mz, mz_send, mz_recv, (mz_ss, mz_rs)),
-        "oz": (oz, oz_send, oz_recv, (oz_ss, oz_rs)),
-        "my": (my, my_send, my_recv, (my_ss, my_rs)),
-        "uz": (lg, uz_send, uz_recv, (uz_ss, uz_rs)),
-    }
+    streams = (
+        (oz, oz_send, oz_recv, (oz_ss, oz_rs)),
+        (mz, mz_send, mz_recv, (mz_ss, mz_rs)),
+        (my, my_send, my_recv, (my_ss, my_rs)),
+        (lg, uz_send, uz_recv, (uz_ss, uz_rs)),
+    )
 
     def ring_copy(name, step, way):
         own, send, recv, sems = streams[name]
@@ -264,13 +175,16 @@
     def update_copy(slot):
         return remote(uy_send.at[slot], uy_recv.at[slot], (uy_ss, uy_rs), slot, pair)
 
-    def update_part(*slots):
+    def update_make(*slots):
         for slot in slots:
             rows = tile_at(ring(DISTANCES[slot]))
             lg_tmp[...] = jnp.dot(left[rows, :], both[plane, :, 0:width], preferred_element_type=F32)
             uy_send[slot] = lg_tmp[other_half, :].astype(BF16)
+            lg[slot] = lg_tmp[own_half, :]
+
+    def update_go(*slots):
+        for slot in slots:
             start(("uy", slot), update_copy(slot))
-            lg[slot] = lg_tmp[own_half, :]
 
     def update_join(*slots):
         for slot in slots:
@@ -296,6 +210,9 @@
                 gather_wait(part, step - 1, way)
             if way in gather_ways(part, step):
                 start(("ag", part, step, way), gather_copy(part, step, way))
+
+    eye = lax.broadcasted_iota(jnp.int32, (TILE, TILE), 0) == lax.broadcasted_iota(jnp.int32, (TILE, TILE), 1)
+    state = {"diagonal": jnp.zeros((TILE, TILE), F32)}
 
     def place(rows, columns, block, turned):
         full[rows, columns] = block
@@ -314,6 +231,8 @@
                         else packed_y[chunk, at - RING_FIRST : at - RING_FIRST + TILE]
                     )
                     place(tile_at(chunk), tile_at(lax.rem(chunk + offset, RING)), block, offset > 0)
+                    if offset == 0:
+                        state["diagonal"] = state["diagonal"] + jnp.where(eye, block.astype(F32), 0.0)
 
     def unpack_far(*distances):
         for distance in distances:
@@ -331,14 +250,14 @@
         return remote(swap_send, swap_recv, (pair_ss, pair_rs), 0, pair)
 
     def swap_start():
-        swap_send[...] = ring_total("oz").astype(BF16)
+        swap_send[...] = ring_total(OZ).astype(BF16)
         start("swap", swap_copy())
 
     def total_y():
-        packed_y[z] = ring_total("my").astype(BF16)
+        packed_y[z] = ring_total(MY).astype(BF16)
 
     def total_z():
-        mz[7] = ring_total("mz")
+        mz[7] = ring_total(MZ)
 
     def swap_done():
         received("swap", swap_copy())
@@ -348,19 +267,15 @@
         for way in gather_ways(part, 3):
             gather_wait(part, 3, way)
 
-    state = {}
+    on_diagonal = (
+        lax.broadcasted_iota(jnp.int32, (TILE, width), 0) + z * TILE
+        == lax.broadcasted_iota(jnp.int32, (TILE, width), 1)
+    )
 
     def center():
-        eye = lax.broadcasted_iota(jnp.int32, (TILE, TILE), 0) == lax.broadcasted_iota(jnp.int32, (TILE, TILE), 1)
-        tiles = [slice(at, at + TILE) for at in range(0, width, TILE)]
-        diagonal = jnp.zeros((TILE, TILE), F32)
-        for at in tiles:
-            diagonal = diagonal + jnp.where(eye, full[at, at].astype(F32), 0.0)
-        trace = jnp.sum(jnp.sum(diagonal, axis=0, keepdims=True), axis=1, keepdims=True)
+        trace = jnp.sum(jnp.sum(state["diagonal"], axis=0, keepdims=True), axis=1, keepdims=True)
         mean = trace / width
         inverse = 0.25 / (2.0 * mean + EPS)
-        for at in tiles:
-            full[at, at] = (full[at, at].astype(F32) - jnp.where(eye, mean, 0.0)).astype(BF16)
         c = (5.0 - DAMP) * 0.25 - mean * inverse
         c2 = c * c
         c3 = c2 * c
@@ -374,12 +289,16 @@
             1.25 - 6.0 * c,
         ]
         state["inverse"] = inverse
-        state["rows"] = state["value"] = full[tile_at(z), :].astype(F32) * inverse
+        state["shift"] = mean * inverse
+        rows = full[tile_at(z), :].astype(F32)
+        state["rows"] = state["value"] = (rows - jnp.where(on_diagonal, mean, 0.0)) * inverse
 
     def newton(*powers):
         for power in powers:
+            value = state["value"].astype(BF16)
             state["value"] = (
-                jnp.dot(state["value"].astype(BF16), full[...], preferred_element_type=F32) * state["inverse"]
+                jnp.dot(value, full[...], preferred_element_type=F32) * state["inverse"]
+                - value.astype(F32) * state["shift"]
                 + state["coefficients"][power] * state["rows"]
             )
 
@@ -387,39 +306,117 @@
         return remote(root_rows.at[other_half], root_recv, (pair_ss, pair_rs), 1, pair)
 
     def root_send():
-        on_diagonal = (
-            lax.broadcasted_iota(jnp.int32, (TILE, width), 0) + z * TILE
-            == lax.broadcasted_iota(jnp.int32, (TILE, width), 1)
-        )
         root_rows[...] = (state["value"] + jnp.where(on_diagonal, state["coefficients"][0], 0.0)).astype(BF16)
         start("root", root_copy())
         roots[plane] = root_rows[own_half, :]
 
     def update_final():
-        total = ring_total("uz").astype(BF16)
+        total = ring_total(UZ).astype(BF16)
         update_out[...] = jnp.dot(total, right[...], preferred_element_type=F32) / (RING * PLANES)
 
     def roots_final():
         received("root", root_copy())
         roots[other_plane] = root_recv[...]
         own_at = pl.ds(pl.multiple_of(group * half, half), half)
-        for side, stale, out in ((0, left, left_out), (1, right, right_out)):
+        for side, stale in ((0, left), (1, right)):
             hits = jnp.int32(0)
             for owner in range(step_ref.shape[0]):
                 hits = hits + (step_ref[owner] == 2 * column + side).astype(jnp.int32)
-            out[0] = jnp.where(jnp.full((half, width), hits) > 0, roots[side], stale[own_at, :])
+            roots_out[side] = jnp.where(jnp.full((half, width), hits) > 0, roots[side], stale[own_at, :])
 
     pl.semaphore_wait(barrier, 3)
-    operations = {
-        operation.__name__: operation
-        for operation in (
-            others, mines, statistic, join, ring_step, load_wait, update_part, update_join, swap_start, swap_done,
-            total_y, total_z, gather_step, gather_done, unpack, unpack_far, center, newton, root_send,
-            update_final, roots_final,
-        )
-    }
-    for name, *values in SCHEDULE:
-        operations[name](*values)
+    others(0)
+    ring_step(OZ, 0)
+    mines(0)
+    ring_step(MZ, 0)
+    others(1)
+    mines(1)
+    others(2)
+    mines(2)
+    join(0)
+    ring_step(MY, 0)
+    others(3)
+    mines(3)
+    others(4)
+    mines(4)
+    ring_step(OZ, 1)
+    ring_step(MZ, 1)
+    others(5)
+    mines(5)
+    others(6)
+    mines(6)
+    others(7)
+    mines(7)
+    load_wait(2)
+    update_make(0)
+    update_make(1)
+    update_make(2)
+    join(1, 2)
+    ring_step(MY, 1)
+    ring_step(OZ, 2)
+    ring_step(MZ, 2)
+    update_make(3)
+    update_make(4)
+    update_make(5)
+    join(3, 4)
+    ring_step(MY, 2)
+    join(5, 6)
+    update_go(0)
+    ring_step(OZ, 3)
+    ring_step(MZ, 3)
+    update_make(6)
+    update_make(7)
+    ring_step(MY, 3)
+    swap_start()
+    update_go(1)
+    update_go(2)
+    update_go(3)
+    update_go(4)
+    update_go(5)
+    update_go(6)
+    update_go(7)
+    join(7)
+    total_y()
+    gather_step(0, 0)
+    total_z()
+    swap_done()
+    gather_step(1, 0)
+    update_join(0)
+    ring_step(UZ, 0)
+    unpack(0, 0)
+    unpack(1, 0)
+    gather_step(0, 1)
+    unpack(0, 1, -1)
+    gather_step(1, 1)
+    unpack(1, 1, -1)
+    gather_step(0, 2)
+    unpack(0, 2, -2)
+    gather_step(1, 2)
+    update_join(1, 2)
+    ring_step(UZ, 1)
+    unpack(1, 2, -2)
+    gather_step(0, 3)
+    unpack(0, 3, -3)
+    gather_step(1, 3)
+    unpack(1, 3, -3)
+    update_join(3, 4)
+    ring_step(UZ, 2)
+    gather_done(0)
+    unpack(0, 4)
+    unpack_far(0, 1, 2, 3)
+    gather_done(1)
+    unpack(1, 4)
+    center()
+    newton(5, 4, 3)
+    update_join(5, 6)
+    ring_step(UZ, 3)
+    newton(2, 1)
+    root_send()
+    load_wait(4)
+    update_join(7)
+    load_wait(3)
+    update_final()
+    roots_final()
 
     for copy in started:
         copy.wait_send()
@@ -435,15 +432,14 @@
     def ring_buffers(rows, columns):
         return [pltpu.VMEM((4, 2, rows, columns), BF16)] * 2
 
-    update, left_roots, right_roots = pl.pallas_call(
+    update, both_roots = pl.pallas_call(
         kernel,
         out_shape=(
             jax.ShapeDtypeStruct((half, width), F32),
-            jax.ShapeDtypeStruct((1, half, width), BF16),
-            jax.ShapeDtypeStruct((1, half, width), BF16),
+            jax.ShapeDtypeStruct((PLANES, half, width), BF16),
         ),
         in_specs=[hbm] * 4,
-        out_specs=(vmem, vmem, vmem),
+        out_specs=(vmem, vmem),
         scratch_shapes=[
             pltpu.VMEM((2, width, width + PACKED - TILE), BF16),
             pltpu.VMEM((width, width), BF16),
@@ -481,7 +477,7 @@
         ),
         name="shampoo",
     )(step_matrix, grad_parts, stale_left, stale_right)
-    return params.astype(F32) - STEP_SIZE * update, left_roots, right_roots
+    return params.astype(F32) - STEP_SIZE * update, both_roots[:1], both_roots[1:]
 
 
 def solution(mesh):

time: 67.5 us -> 62.7 us (0.929)
  Pallas kernels: 64.1 us -> 59.8 us
    pallas_call x1, Pallas kernels: 64.1 us -> 59.8 us  [per_device(): pl.pallas_call(kernel, out_shape=(jax.ShapeDtypeStruct((half, width), F32...]
    unnamed x6 -> x4, local copies, waits for them, and re-layouts: 1.96 us -> 0.65 us
    slice x0 -> x1, local copies, waits for them, and re-layouts: none -> 0.71 us  [per_device(): both_roots[1:]]
where the time goes in v3:
time: 62.7 us; the launch traced here: 62.6 us
  Pallas kernels  59.8 us (95%)
  local copies, waits for them, and re-layouts  1.37 us (2%)
  other arithmetic  0.73 us (1%)
  between operations  0.66 us (1%)
    pallas_call x1, Pallas kernels, per_device(): pl.pallas_call(kernel, out_shape=(jax.ShapeDtypeStruct((half, width), F32...  59.8 us

profile of v3, /device:TPU:6, one launch (start us, length us, event | category | flops | bytes accessed | tf_op | source)
XLA Modules:
  0.0 62.6 jit_solution(5748091801388701080)
XLA Ops:
  0.6 0.0 copy-start
  0.6 0.6 %copy-done = s32[16]{0:T(128)S(1)} copy-done((s32[16]{0:T(128)S(1)}, s32[16]{0:T(128)}, u32[]{:S(2)}) %copy-start) | copy-done | bytes 88
  1.3 0.0 copy-start.1
  1.3 59.8 %shampoo.1 = (f32[64,1024]{1,0:T(8,128)S(1)}, bf16[2,64,1024]{2,1,0:T(8,128)(2,1)S(1)}) custom-call(s32[16]{0:T(128)S(1)} %copy-done, bf16[1,1024,1024]{2,1,0:T(8,128)(2,1)} %g_hbm.1, bf16[1,1024,1024]{2,1,0:T(8,128)(2,1)} %left_hbm.1, bf16[1,1024,1024]{2,1,0:T(8,128)(2,1)} %right_hbm.1), custom_call_target="tpu_custom_call" | custom-call | tf_op jit(solution)/shard_map/shampoo/pallas_call | solution.py:435
  61.1 0.0 copy-done.1
  61.1 0.7 %multiply_subtract_fusion = f32[64,1024]{1,0:T(8,128)} fusion(f32[64,1024]{1,0:T(8,128)S(1)} %get-tuple-element.5, bf16[64,1024]{1,0:T(8,128)(2,1)S(1)} %copy-done.1), kind=kLoop, calls=%fused_computation | loop fusion | flops 196608 | bytes 655360 | tf_op jit(solution)/shard_map/sub | solution.py:480
  61.9 0.7 %fusion = (bf16[1,64,1024]{2,1,0:T(8,128)(2,1)}, bf16[1,64,1024]{2,1,0:T(8,128)(2,1)}) fusion(bf16[2,64,1024]{2,1,0:T(8,128)(2,1)S(1)} %get-tuple-element.6), kind=kLoop, calls=%fused_computation.1 | loop fusion | bytes 524288 | tf_op jit(solution)/shard_map/slice | solution.py:480
Async XLA Ops:
  0.6 0.7 %copy-start = (s32[16]{0:T(128)S(1)}, s32[16]{0:T(128)}, u32[]{:S(2)}) copy-start(s32[16]{0:T(128)} %step_hbm.1) | copy-start | bytes 196
  1.3 59.8 %copy-start.1 = (bf16[64,1024]{1,0:T(8,128)(2,1)S(1)}, bf16[64,1024]{1,0:T(8,128)(2,1)}, u32[]{:S(2)}) copy-start(bf16[64,1024]{1,0:T(8,128)(2,1)} %param.6) | copy-start | bytes 393220

commit v4 on v3

--- a/solution.py
+++ b/solution.py
@@ -370,19 +370,19 @@
     swap_start()
     update_go(1)
     update_go(2)
+    join(7)
+    total_y()
+    gather_step(0, 0)
     update_go(3)
+    update_join(0)
+    ring_step(UZ, 0)
     update_go(4)
     update_go(5)
     update_go(6)
     update_go(7)
-    join(7)
-    total_y()
-    gather_step(0, 0)
     total_z()
     swap_done()
     gather_step(1, 0)
-    update_join(0)
-    ring_step(UZ, 0)
     unpack(0, 0)
     unpack(1, 0)
     gather_step(0, 1)

time: 62.7 us -> 62 us (0.989)
  Pallas kernels: 59.8 us -> 59 us
    pallas_call x1, Pallas kernels: 59.8 us -> 59 us  [per_device(): pl.pallas_call(kernel, out_shape=(jax.ShapeDtypeStruct((half, width), F32...]
where the time goes in v4:
time: 62 us; the launch traced here: 61.8 us
  Pallas kernels  59 us (95%)
  local copies, waits for them, and re-layouts  1.37 us (2%)
  other arithmetic  0.73 us (1%)
  between operations  0.66 us (1%)
    pallas_call x1, Pallas kernels, per_device(): pl.pallas_call(kernel, out_shape=(jax.ShapeDtypeStruct((half, width), F32...  59 us

profile of v4, /device:TPU:6, one launch (start us, length us, event | category | flops | bytes accessed | tf_op | source)
XLA Modules:
  0.0 61.8 jit_solution(1132300982226149599)
XLA Ops:
  0.6 0.0 copy-start
  0.6 0.6 %copy-done = s32[16]{0:T(128)S(1)} copy-done((s32[16]{0:T(128)S(1)}, s32[16]{0:T(128)}, u32[]{:S(2)}) %copy-start) | copy-done | bytes 88
  1.3 0.0 copy-start.1
  1.3 59.0 %shampoo.1 = (f32[64,1024]{1,0:T(8,128)S(1)}, bf16[2,64,1024]{2,1,0:T(8,128)(2,1)S(1)}) custom-call(s32[16]{0:T(128)S(1)} %copy-done, bf16[1,1024,1024]{2,1,0:T(8,128)(2,1)} %g_hbm.1, bf16[1,1024,1024]{2,1,0:T(8,128)(2,1)} %left_hbm.1, bf16[1,1024,1024]{2,1,0:T(8,128)(2,1)} %right_hbm.1), custom_call_target="tpu_custom_call" | custom-call | tf_op jit(solution)/shard_map/shampoo/pallas_call | solution.py:435
  60.3 0.0 copy-done.1
  60.3 0.7 %multiply_subtract_fusion = f32[64,1024]{1,0:T(8,128)} fusion(f32[64,1024]{1,0:T(8,128)S(1)} %get-tuple-element.5, bf16[64,1024]{1,0:T(8,128)(2,1)S(1)} %copy-done.1), kind=kLoop, calls=%fused_computation | loop fusion | flops 196608 | bytes 655360 | tf_op jit(solution)/shard_map/sub | solution.py:480
  61.1 0.7 %fusion = (bf16[1,64,1024]{2,1,0:T(8,128)(2,1)}, bf16[1,64,1024]{2,1,0:T(8,128)(2,1)}) fusion(bf16[2,64,1024]{2,1,0:T(8,128)(2,1)S(1)} %get-tuple-element.6), kind=kLoop, calls=%fused_computation.1 | loop fusion | bytes 524288 | tf_op jit(solution)/shard_map/slice | solution.py:480
Async XLA Ops:
  0.6 0.7 %copy-start = (s32[16]{0:T(128)S(1)}, s32[16]{0:T(128)}, u32[]{:S(2)}) copy-start(s32[16]{0:T(128)} %step_hbm.1) | copy-start | bytes 196
  1.3 59.0 %copy-start.1 = (bf16[64,1024]{1,0:T(8,128)(2,1)S(1)}, bf16[64,1024]{1,0:T(8,128)(2,1)}, u32[]{:S(2)}) copy-start(bf16[64,1024]{1,0:T(8,128)(2,1)} %param.6) | copy-start | bytes 393220
